TPU v7x, 256 devices: a whole 4x4x8 slice. The times are simulated.
256 devices in a mesh: lat: 8 (over y_hi, x), lon: 32 (over z, y_lo, core).
Axes of the slice: x: 4, y: 4 (y_hi: 2, y_lo: 2; y = y_hi * 2 + y_lo), z: 8, core: 2. Of those that a mesh axis runs over, the one named last changes fastest.
Arguments:
- adj_height: float32 [3, 3, 128, 24576], P(None, None, 'lat', 'lon'), may hold values from -6 to 6
- adj_east: float32 [3, 3, 128, 24576], P(None, None, 'lat', 'lon'), may hold values from -6 to 6
- adj_north: float32 [3, 3, 128, 24576], P(None, None, 'lat', 'lon'), may hold values from -6 to 6
- flow_east: float32 [3, 3, 128, 24576], P(None, None, 'lat', 'lon'), may hold values from -6 to 6
- flow_north: float32 [3, 3, 128, 24576], P(None, None, 'lat', 'lon'), may hold values from -6 to 6
- depth: float32 [3, 3, 128, 24576], P(None, None, 'lat', 'lon'), may hold values from 0.5 to 2
- friction: float32 [128, 24576], P('lat', 'lon'), may hold values from 0.2 to 2
- wet_dry: int32 [128, 24576], P('lat', 'lon'), may hold values 0 or 1
- sea_mask: int32 [128, 24576], P('lat', 'lon'), may hold values 0 or 1
- grad_depth: float32 [3, 3, 128, 24576], P(None, None, 'lat', 'lon'), may hold values from -6 to 6
- grad_friction: float32 [128, 24576], P('lat', 'lon'), may hold values from -6 to 6
- gauss_index: int32 [2048, 4096], P('lat', 'lon'), may hold values from 0 to 110591, as said below
- legendre: bfloat16 [256, 2048, 2048], P('lon', None, 'lat'), may hold values from -0.125 to 0.125
- love_gain: float32 [2048], replicated, may hold values from 0.3 to 3
Outputs:
- new_height: float32 [3, 3, 128, 24576], P(None, None, 'lat', 'lon')
- new_east: float32 [3, 3, 128, 24576], P(None, None, 'lat', 'lon')
- new_north: float32 [3, 3, 128, 24576], P(None, None, 'lat', 'lon')
- depth_grad: float32 [3, 3, 128, 24576], P(None, None, 'lat', 'lon')
- friction_grad: float32 [128, 24576], P('lat', 'lon')
Inputs may be any that keep to these rules, and one draw needn't show every extreme that they name: `gauss_index`: each entry names a node of the cells of the same tile, as its position among that tile's 9 * 16 * 768 nodes flattened in the order latitude node, longitude node, cell row, cell column. The node lies in cell row (the point's latitude within its tile) // ((2048 / 8) / 16) of the tile.
All inputs are finite; a program needn't handle non-finite values. No bound on the sum of `wet_dry` or of `sea_mask` on one device may be relied on, other than what follows from the above.
Results may differ from a plain program's by a relative error of at most 0.00085.
Values may be sent and summed in bfloat16 or wider, within the bound.
No kernel may reach another device: no remote copies, remote signals or barrier semaphores. Data moves between devices by JAX's collectives and lax.ppermute only.
A program may use at most 128 MiB of HBM per device.

v0:
```python
import math

import jax
import jax.numpy as jnp
from jax import lax
from jax.sharding import PartitionSpec as P

stencil = ((-1.5, 2.0, -0.5), (-0.5, 0.0, 0.5), (0.5, -2.0, 1.5))
quadrature = (1.0 / 3.0, 4.0 / 3.0, 1.0 / 3.0)
penalty = 1.5
courant = 0.3


def extended(block, sides, width, periodic):
    for axis, dim in sides:
        count = lax.axis_size(axis)
        forward = [(i, i + 1) for i in range(count - 1)]
        if periodic:
            forward.append((count - 1, 0))
        backward = [(target, source) for source, target in forward]
        low = lax.ppermute(
            lax.slice_in_dim(block, block.shape[dim] - width, None, axis=dim), axis, forward
        )
        high = lax.ppermute(lax.slice_in_dim(block, 0, width, axis=dim), axis, backward)
        block = jnp.concatenate([low, block, high], axis=dim)
    return block


def inner_part(layers):
    return [
        stencil[target][0] * layers[0]
        + stencil[target][1] * layers[1]
        + stencil[target][2] * layers[2]
        for target in range(3)
    ]


def lon_apply(stacked):
    layers = [stacked[:, :, column] for column in range(3)]
    traces = jnp.stack((layers[0], layers[2]), axis=0)
    padded = extended(traces, (("lon", 4),), 1, True)
    previous = padded[1, :, :, :, :-2]
    following = padded[0, :, :, :, 2:]
    result = inner_part(layers)
    result[0] = result[0] + penalty * (layers[0] - previous)
    result[2] = result[2] + penalty * (following - layers[2])
    return jnp.stack(result, axis=2)


def lat_apply(stacked):
    layers = [stacked[:, column] for column in range(3)]
    traces = jnp.stack((layers[0], layers[2]), axis=0)
    padded = extended(traces, (("lat", 3),), 1, False)
    previous = padded[1, :, :, :-2, :]
    following = padded[0, :, :, 2:, :]
    result = inner_part(layers)
    result[0] = result[0] + penalty * (layers[0] - previous)
    result[2] = result[2] + penalty * (following - layers[2])
    return jnp.stack(result, axis=1)


def lon_transpose(stacked):
    weights = jnp.array(quadrature, jnp.float32).reshape(1, 1, 3, 1, 1)
    return -weights * lon_apply(stacked / weights)


def lat_transpose(stacked):
    weights = jnp.array(quadrature, jnp.float32).reshape(1, 3, 1, 1, 1)
    return -weights * lat_apply(stacked / weights)


def contract_last(left_side, right_side):
    return lax.dot_general(
        left_side,
        right_side,
        (((1,), (1,)), ((), ())),
        precision=lax.Precision.HIGHEST,
        preferred_element_type=jnp.float32,
    )


def contract_first(left_side, right_side):
    return lax.dot_general(
        left_side,
        right_side,
        (((0,), (0,)), ((), ())),
        precision=lax.Precision.HIGHEST,
        preferred_element_type=jnp.float32,
    )


def wave_tables(mode_count, lon_first, lon_count, circle):
    wave_numbers = jnp.arange(mode_count, dtype=jnp.int32)
    places = lon_first + jnp.arange(lon_count, dtype=jnp.int32)
    phase_index = wave_numbers[:, None] * places[None, :] % circle
    angle_table = phase_index.astype(jnp.float32) * (2.0 * math.pi / circle)
    return (jnp.cos(angle_table), jnp.sin(angle_table))


def sample_block(inputs):
    block_index, block_nodes = inputs
    node_ids = jnp.arange(block_nodes.shape[0], dtype=jnp.int32)
    matches = block_index[:, None] == node_ids[None, :]
    return jnp.sum(jnp.where(matches, block_nodes[None, :], 0.0), axis=1)


def loading(source, gauss_index, legendre, love_gain):
    lon_devices = lax.axis_size("lon")
    grid_rows, grid_cols = gauss_index.shape
    circle = grid_cols * lon_devices
    mode_local = legendre.shape[0]
    degree_total = love_gain.shape[0]
    norm_factor = math.sqrt(2.0 / circle)
    cell_rows = source.shape[2]
    cell_cols = source.shape[3]
    block_nodes = 9 * cell_cols
    node_blocks = (
        source.reshape(9, cell_rows, cell_cols).transpose(1, 0, 2).reshape(cell_rows, block_nodes)
    )
    local_index = gauss_index // (cell_rows * cell_cols) * cell_cols + gauss_index % cell_cols
    index_blocks = local_index.reshape(cell_rows, grid_rows // cell_rows * grid_cols)
    sampled = lax.map(sample_block, (index_blocks, node_blocks)).reshape(grid_rows, grid_cols)
    lon_first = lax.axis_index("lon") * grid_cols
    cosine_table, sine_table = wave_tables(
        mode_local * lax.axis_size("lon"), lon_first, grid_cols, circle
    )
    real_part = norm_factor * contract_last(cosine_table, sampled)
    imag_part = -norm_factor * contract_last(sine_table, sampled)
    spectrum = lax.psum_scatter(
        jnp.stack((real_part, imag_part), axis=1), "lon", scatter_dimension=0, tiled=True
    )
    rounded = spectrum.astype(jnp.bfloat16)
    partial_sums = jnp.einsum("kja,kla->kjl", rounded, legendre, preferred_element_type=jnp.float32)
    own_modes = lax.axis_index("lon") * mode_local + jnp.arange(mode_local, dtype=jnp.int32)
    coeffs = lax.psum(partial_sums, "lat")
    degrees = jnp.arange(degree_total, dtype=jnp.int32)
    live_mask = (degrees[None, :] >= own_modes[:, None]).astype(jnp.float32)
    scaled = (coeffs * (live_mask * love_gain[None, :])[:, None, :]).astype(jnp.bfloat16)
    synthesis = jnp.einsum("kjl,kla->kja", scaled, legendre, preferred_element_type=jnp.float32)
    mode_piece = lax.all_gather(synthesis, "lon", axis=0, tiled=True)
    cosine_table, sine_table = wave_tables(mode_piece.shape[0], lon_first, grid_cols, circle)
    grid_field = norm_factor * (
        contract_first(mode_piece[:, 0, :], cosine_table)
        - contract_first(mode_piece[:, 1, :], sine_table)
    )
    field_blocks = grid_field.reshape(cell_rows, grid_rows // cell_rows * grid_cols)

    def gather_block(inputs):
        block_index, block_field = inputs
        node_ids = jnp.arange(block_nodes, dtype=jnp.int32)
        matches = block_index[:, None] == node_ids[None, :]
        return jnp.sum(jnp.where(matches, block_field[:, None], 0.0), axis=0)

    summed = lax.map(gather_block, (index_blocks, field_blocks))
    return summed.reshape(cell_rows, 9, cell_cols).transpose(1, 0, 2).reshape(source.shape)


def local(
    adj_height,
    adj_east,
    adj_north,
    flow_east,
    flow_north,
    depth,
    friction,
    wet_dry,
    sea_mask,
    grad_depth,
    grad_friction,
    gauss_index,
    legendre,
    love_gain,
):
    wet_cells = (wet_dry * sea_mask).astype(jnp.float32)
    lon_terms = lon_transpose(jnp.stack((wet_cells * adj_east, wet_cells * adj_height), axis=0))
    lat_terms = lat_transpose(jnp.stack((wet_cells * adj_north, wet_cells * adj_height), axis=0))
    lon_height = lon_terms[1]
    lat_height = lat_terms[1]
    source = lon_terms[0] + lat_terms[0]
    loaded = loading(source, gauss_index, legendre, love_gain)
    new_height = adj_height - courant * (source - loaded)
    retain = wet_cells * (1.0 - courant * friction)
    new_east = retain * adj_east - courant * depth * wet_cells * lon_height
    new_north = retain * adj_north - courant * depth * wet_cells * lat_height
    depth_grad = grad_depth - courant * wet_cells * (
        flow_east * lon_height + flow_north * lat_height
    )
    friction_grad = grad_friction - courant * wet_cells * jnp.sum(
        flow_east * adj_east + flow_north * adj_north, axis=(0, 1)
    )
    return (new_height, new_east, new_north, depth_grad, friction_grad)


def solution(mesh):
    in_specs = (
        P(None, None, "lat", "lon"),
        P(None, None, "lat", "lon"),
        P(None, None, "lat", "lon"),
        P(None, None, "lat", "lon"),
        P(None, None, "lat", "lon"),
        P(None, None, "lat", "lon"),
        P("lat", "lon"),
        P("lat", "lon"),
        P("lat", "lon"),
        P(None, None, "lat", "lon"),
        P("lat", "lon"),
        P("lat", "lon"),
        P("lon", None, "lat"),
        P(),
    )
    out_specs = (
        P(None, None, "lat", "lon"),
        P(None, None, "lat", "lon"),
        P(None, None, "lat", "lon"),
        P(None, None, "lat", "lon"),
        P("lat", "lon"),
    )
    return jax.shard_map(local, mesh=mesh, in_specs=in_specs, out_specs=out_specs, check_vma=False)
```

profile of v0, /device:TPU:1, one launch (start us, length us, event | category | flops | bytes accessed | tf_op | source)
XLA Modules:
  0.0 776.5 jit_solution(16669751921361866414)
XLA Ops:
  7.2 1.5 add_reduce_fusion
  8.8 1.5 multiply_subtract_fusion.3
  12.8 3.9 collective-permute-start.2
  18.8 2.1 collective-permute-start
  21.3 1.9 collective-permute-done
  23.3 2.2 collective-permute-done.1
  28.0 125.1 %while.20 = (s32[]{:T(128)}, f32[16,2048]{1,0:T(8,128)S(1)}, s32[16,2048]{1,0:T(8,128)S(1)}, f32[16,6912]{1,0:T(8,128)S(1)}, s32[]{:T(128)}, /*index=5*/s32[]{:T(128)}) while((s32[]{:T(128)}, f32[16,2048]{1,0:T(8,128)S(1)}, s32[16,2048]{1,0:T(8,128)S(1)}, f32[16,6912]{1,0:T(8,128)S(1)}, s32[]{:T(128)}, /*index=5*/s32[]{:T(128)}) %tuple.63), condition=%wide.region_2.3_spmd, body=%wide.region_0.2_spmd.sunk | while | flops 42465280 | bytes 132177 | solution.py:122
  28.1 7.5 select_reduce_fusion.4
  35.9 7.5 select_reduce_fusion.4
  43.7 7.5 select_reduce_fusion.4
  51.5 7.5 select_reduce_fusion.4
  59.4 7.5 select_reduce_fusion.4
  67.2 7.5 select_reduce_fusion.4
  75.0 7.5 select_reduce_fusion.4
  82.8 7.5 select_reduce_fusion.4
  90.6 7.5 select_reduce_fusion.4
  98.5 7.5 select_reduce_fusion.4
  106.3 7.5 select_reduce_fusion.4
  114.1 7.5 select_reduce_fusion.4
  121.9 7.5 select_reduce_fusion.4
  129.7 7.5 select_reduce_fusion.4
  137.6 7.5 select_reduce_fusion.4
  145.4 7.5 select_reduce_fusion.4
  156.0 117.8 %reduce-scatter.2.cloned.1.call-done = f32[8,2,256]{2,0,1:T(8,128)} async-done(((f32[256,2,256]{2,0,1:T(8,128)}), f32[8,2,256]{2,0,1:T(8,128)}) %reduce-scatter.2.cloned.1.call-update) | async-done | bytes 16400 | tf_op jit(solution)/shard_map/reduce_scatter | solution.py:129
  274.5 6.3 fusion.56
  281.5 84.9 %all-reduce.2.cloned.1.call-done = f32[8,2,2048]{2,1,0:T(2,128)} async-done(((f32[8,2,2048]{2,1,0:T(2,128)}), f32[8,2,2048]{2,1,0:T(2,128)}) %all-reduce.2.cloned.1.call-update) | async-done | bytes 131088 | tf_op jit(solution)/shard_map/psum | solution.py:135
  366.4 4.6 fusion.47
  371.0 41.0 %all_gather.3 = f32[256,2,256]{2,1,0:T(2,128)S(1)} all-gather(f32[8,2,256]{2,1,0:T(2,128)S(1)} %fusion.47), channel_id=1, replica_groups=mesh['lat'=8,'lon'=32] {'lon'}, dimensions={0}, use_global_device_ids=true | all-gather | bytes 540672 | tf_op jit(solution)/shard_map/all_gather | solution.py:140
  413.5 1.6 fusion.2
  416.0 346.7 %while.21 = (s32[]{:T(128)}, f32[16,6912]{1,0:T(8,128)}, s32[16,2048]{1,0:T(8,128)S(1)}, f32[16,2048]{1,0:T(8,128)S(1)}, s32[]{:T(128)}, /*index=5*/s32[]{:T(128)}) while((s32[]{:T(128)}, f32[16,6912]{1,0:T(8,128)}, s32[16,2048]{1,0:T(8,128)S(1)}, f32[16,2048]{1,0:T(8,128)S(1)}, s32[]{:T(128)}, /*index=5*/s32[]{:T(128)}) %tuple.64), condition=%wide.region_7.8_spmd, body=%wide.region_5.7_spmd.sunk | while | flops 42460416 | bytes 187473 | solution.py:154
  416.1 19.9 %select_reduce_fusion.5 = f32[6912]{0:T(1024)S(1)} fusion(f32[2048]{0:T(1024)S(1)} %bitcast.158, s32[2048]{0:T(1024)S(1)} %bitcast.159), kind=kLoop, calls=%fused_computation.clone.1 | loop fusion | flops 42460416 | bytes 44032 | tf_op jit(solution)/shard_map/while/body/eval_jaxpr/reduce_sum | solution.py:152
  436.0 1.7 dynamic_update_slice.11
  437.8 19.9 %select_reduce_fusion.5 = f32[6912]{0:T(1024)S(1)} fusion(f32[2048]{0:T(1024)S(1)} %bitcast.158, s32[2048]{0:T(1024)S(1)} %bitcast.159), kind=kLoop, calls=%fused_computation.clone.1 | loop fusion | flops 42460416 | bytes 44032 | tf_op jit(solution)/shard_map/while/body/eval_jaxpr/reduce_sum | solution.py:152
  457.7 1.7 dynamic_update_slice.11
  459.4 19.9 %select_reduce_fusion.5 = f32[6912]{0:T(1024)S(1)} fusion(f32[2048]{0:T(1024)S(1)} %bitcast.158, s32[2048]{0:T(1024)S(1)} %bitcast.159), kind=kLoop, calls=%fused_computation.clone.1 | loop fusion | flops 42460416 | bytes 44032 | tf_op jit(solution)/shard_map/while/body/eval_jaxpr/reduce_sum | solution.py:152
  479.3 1.7 dynamic_update_slice.11
  481.1 19.9 %select_reduce_fusion.5 = f32[6912]{0:T(1024)S(1)} fusion(f32[2048]{0:T(1024)S(1)} %bitcast.158, s32[2048]{0:T(1024)S(1)} %bitcast.159), kind=kLoop, calls=%fused_computation.clone.1 | loop fusion | flops 42460416 | bytes 44032 | tf_op jit(solution)/shard_map/while/body/eval_jaxpr/reduce_sum | solution.py:152
  501.0 1.7 dynamic_update_slice.11
  502.8 19.9 %select_reduce_fusion.5 = f32[6912]{0:T(1024)S(1)} fusion(f32[2048]{0:T(1024)S(1)} %bitcast.158, s32[2048]{0:T(1024)S(1)} %bitcast.159), kind=kLoop, calls=%fused_computation.clone.1 | loop fusion | flops 42460416 | bytes 44032 | tf_op jit(solution)/shard_map/while/body/eval_jaxpr/reduce_sum | solution.py:152
  522.7 1.7 dynamic_update_slice.11
  524.4 19.9 %select_reduce_fusion.5 = f32[6912]{0:T(1024)S(1)} fusion(f32[2048]{0:T(1024)S(1)} %bitcast.158, s32[2048]{0:T(1024)S(1)} %bitcast.159), kind=kLoop, calls=%fused_computation.clone.1 | loop fusion | flops 42460416 | bytes 44032 | tf_op jit(solution)/shard_map/while/body/eval_jaxpr/reduce_sum | solution.py:152
  544.3 1.7 dynamic_update_slice.11
  546.1 19.9 %select_reduce_fusion.5 = f32[6912]{0:T(1024)S(1)} fusion(f32[2048]{0:T(1024)S(1)} %bitcast.158, s32[2048]{0:T(1024)S(1)} %bitcast.159), kind=kLoop, calls=%fused_computation.clone.1 | loop fusion | flops 42460416 | bytes 44032 | tf_op jit(solution)/shard_map/while/body/eval_jaxpr/reduce_sum | solution.py:152
  566.0 1.7 dynamic_update_slice.11
  567.8 19.9 %select_reduce_fusion.5 = f32[6912]{0:T(1024)S(1)} fusion(f32[2048]{0:T(1024)S(1)} %bitcast.158, s32[2048]{0:T(1024)S(1)} %bitcast.159), kind=kLoop, calls=%fused_computation.clone.1 | loop fusion | flops 42460416 | bytes 44032 | tf_op jit(solution)/shard_map/while/body/eval_jaxpr/reduce_sum | solution.py:152
  587.7 1.7 dynamic_update_slice.11
  589.4 19.9 %select_reduce_fusion.5 = f32[6912]{0:T(1024)S(1)} fusion(f32[2048]{0:T(1024)S(1)} %bitcast.158, s32[2048]{0:T(1024)S(1)} %bitcast.159), kind=kLoop, calls=%fused_computation.clone.1 | loop fusion | flops 42460416 | bytes 44032 | tf_op jit(solution)/shard_map/while/body/eval_jaxpr/reduce_sum | solution.py:152
  609.4 1.7 dynamic_update_slice.11
  611.1 19.9 %select_reduce_fusion.5 = f32[6912]{0:T(1024)S(1)} fusion(f32[2048]{0:T(1024)S(1)} %bitcast.158, s32[2048]{0:T(1024)S(1)} %bitcast.159), kind=kLoop, calls=%fused_computation.clone.1 | loop fusion | flops 42460416 | bytes 44032 | tf_op jit(solution)/shard_map/while/body/eval_jaxpr/reduce_sum | solution.py:152
  631.0 1.7 dynamic_update_slice.11
  632.8 19.9 %select_reduce_fusion.5 = f32[6912]{0:T(1024)S(1)} fusion(f32[2048]{0:T(1024)S(1)} %bitcast.158, s32[2048]{0:T(1024)S(1)} %bitcast.159), kind=kLoop, calls=%fused_computation.clone.1 | loop fusion | flops 42460416 | bytes 44032 | tf_op jit(solution)/shard_map/while/body/eval_jaxpr/reduce_sum | solution.py:152
  652.7 1.7 dynamic_update_slice.11
  654.4 19.9 %select_reduce_fusion.5 = f32[6912]{0:T(1024)S(1)} fusion(f32[2048]{0:T(1024)S(1)} %bitcast.158, s32[2048]{0:T(1024)S(1)} %bitcast.159), kind=kLoop, calls=%fused_computation.clone.1 | loop fusion | flops 42460416 | bytes 44032 | tf_op jit(solution)/shard_map/while/body/eval_jaxpr/reduce_sum | solution.py:152
  674.4 1.7 dynamic_update_slice.11
  676.1 19.9 %select_reduce_fusion.5 = f32[6912]{0:T(1024)S(1)} fusion(f32[2048]{0:T(1024)S(1)} %bitcast.158, s32[2048]{0:T(1024)S(1)} %bitcast.159), kind=kLoop, calls=%fused_computation.clone.1 | loop fusion | flops 42460416 | bytes 44032 | tf_op jit(solution)/shard_map/while/body/eval_jaxpr/reduce_sum | solution.py:152
  696.0 1.7 dynamic_update_slice.11
  697.8 19.9 %select_reduce_fusion.5 = f32[6912]{0:T(1024)S(1)} fusion(f32[2048]{0:T(1024)S(1)} %bitcast.158, s32[2048]{0:T(1024)S(1)} %bitcast.159), kind=kLoop, calls=%fused_computation.clone.1 | loop fusion | flops 42460416 | bytes 44032 | tf_op jit(solution)/shard_map/while/body/eval_jaxpr/reduce_sum | solution.py:152
  717.7 1.7 dynamic_update_slice.11
  719.5 19.9 %select_reduce_fusion.5 = f32[6912]{0:T(1024)S(1)} fusion(f32[2048]{0:T(1024)S(1)} %bitcast.158, s32[2048]{0:T(1024)S(1)} %bitcast.159), kind=kLoop, calls=%fused_computation.clone.1 | loop fusion | flops 42460416 | bytes 44032 | tf_op jit(solution)/shard_map/while/body/eval_jaxpr/reduce_sum | solution.py:152
  739.4 1.7 dynamic_update_slice.11
  741.1 19.9 %select_reduce_fusion.5 = f32[6912]{0:T(1024)S(1)} fusion(f32[2048]{0:T(1024)S(1)} %bitcast.158, s32[2048]{0:T(1024)S(1)} %bitcast.159), kind=kLoop, calls=%fused_computation.clone.1 | loop fusion | flops 42460416 | bytes 44032 | tf_op jit(solution)/shard_map/while/body/eval_jaxpr/reduce_sum | solution.py:152
  761.0 1.7 dynamic_update_slice.11
  762.8 2.0 reshape.95
  766.2 3.1 multiply_subtract_fusion
  (146 shorter events, 20.9 us)
Async XLA Ops:
  7.2 20.4 %copy-start.6 = (f32[3]{0:T(128)S(1)}, f32[3]{0:T(128)}, u32[]{:S(2)}) copy-start(f32[3]{0:T(128)} %constant.107) | copy-start | bytes 40
  7.2 13.9 %copy-start.3 = (s32[256,128]{1,0:T(8,128)S(1)}, s32[256,128]{1,0:T(8,128)}, u32[]{:S(2)}) copy-start(s32[256,128]{1,0:T(8,128)} %param.31) | copy-start | bytes 393220
  7.2 266.6 %reduce-scatter.2.cloned.1.call-start = ((), (), s32[]{:S(2)}) async-start(), calls=%async_computation.1 | async-start | bytes 540672 | tf_op jit(solution)/shard_map/reduce_scatter | solution.py:129
  12.8 13.8 %collective-permute-start.2 = (f32[2,2,3,1,768]{4,3,1,2,0:T(1,128)S(1)}, f32[2,2,3,1,768]{4,3,1,2,0:T(1,128)S(1)}, u32[]{:S(2)}, u32[]{:S(2)}) collective-permute-start(f32[2,2,3,1,768]{4,3,1,2,0:T(1,128)S(1)} %get-tuple-element.84), channel_id=1, source_target_pairs={{0,32},{32,64},{64,96},{96,128},{128,160},{160,192},{192,224},{1,3... | collective-permute-start | bytes 110600 | tf_op jit(solution)/shard_map/ppermute | solution.py:21
  16.7 9.8 %collective-permute-start.3 = (f32[2,2,3,1,768]{4,3,1,2,0:T(1,128)S(1)}, f32[2,2,3,1,768]{4,3,1,2,0:T(1,128)}, u32[]{:S(2)}, u32[]{:S(2)}) collective-permute-start(f32[2,2,3,1,768]{4,3,1,2,0:T(1,128)S(1)} %get-tuple-element.85), channel_id=1, source_target_pairs={{32,0},{64,32},{96,64},{128,96},{160,128},{192,160},{224,192},{33,... | collective-permute-start | bytes 110600 | tf_op jit(solution)/shard_map/ppermute | solution.py:24
  18.1 137.9 %copy-start.5 = (f32[2048]{0:T(1024)S(1)}, f32[2048]{0:T(1024)}, u32[]{:S(2)}) copy-start(f32[2048]{0:T(1024)} %param.33) | copy-start | bytes 24580
  18.8 4.4 collective-permute-start
  20.9 4.5 collective-permute-start.1
  27.8 253.0 %copy-start.4 = (f32[16,768]{1,0:T(8,128)S(1)}, f32[16,768]{1,0:T(8,128)}, u32[]{:S(2)}) copy-start(f32[16,768]{1,0:T(8,128)} %param.26) | copy-start | bytes 147460
  155.6 210.8 %all-reduce.2.cloned.1.call-start = ((), (), s32[]{:S(2)}) async-start(), calls=%async_computation.2 | async-start | bytes 262144 | tf_op jit(solution)/shard_map/psum | solution.py:135
  281.5 484.7 %copy-start = (f32[3,3,16,768]{3,2,1,0:T(8,128)S(1)}, f32[3,3,16,768]{3,2,1,0:T(8,128)}, u32[]{:S(2)}) copy-start(f32[3,3,16,768]{3,2,1,0:T(8,128)} %param.21) | copy-start | bytes 1327108
  281.5 484.7 %copy-start.1 = (f32[3,3,16,768]{3,2,1,0:T(8,128)S(1)}, f32[3,3,16,768]{3,2,1,0:T(8,128)}, u32[]{:S(2)}) copy-start(f32[3,3,16,768]{3,2,1,0:T(8,128)} %param.22) | copy-start | bytes 1327108
  281.5 484.7 %copy-start.2 = (f32[16,768]{1,0:T(8,128)S(1)}, f32[16,768]{1,0:T(8,128)}, u32[]{:S(2)}) copy-start(f32[16,768]{1,0:T(8,128)} %get-tuple-element.91) | copy-start | bytes 147460
Sparse Core Ops, SparseCore 0:
  155.8 118.0 reduce-scatter.1
  281.0 85.3 all-reduce.1
where the time goes:
time: 780 us; the launch traced here: 777 us
  other arithmetic  452 us (58%)
  waiting for transfers between devices  207 us (27%)
  blocking collectives  41 us (5%)
  local copies, waits for them, and re-layouts  38 us (5%)
  matrix products  15.2 us (2%)
  between operations  14.7 us (2%)
  starting transfers between devices  7.82 us (1%)
    reduce_sum x16, other arithmetic, gather_block(): return jnp.sum(jnp.where(matches, block_field[:, None], 0.0), axis=0)  318 us
    reduce_sum x16, other arithmetic, sample_block(): return jnp.sum(jnp.where(matches, block_nodes[None, :], 0.0), axis=1)  120 us
    reduce_scatter x1, waiting for transfers between devices, loading(): lax.psum_scatter(jnp.stack((real_part, imag_part), axis=1), 'lon', scatte...  118 us
    psum x1, waiting for transfers between devices, loading(): coeffs = lax.psum(partial_sums, 'lat')  84.9 us
    all_gather x1, blocking collectives, loading(): mode_piece = lax.all_gather(synthesis, 'lon', axis=0, tiled=True)  41 us
    dynamic_update_slice x16, local copies, waits for them, and re-layouts, loading(): summed = lax.map(gather_block, (index_blocks, field_blocks))  27.5 us
  transfers between devices with their start and end apart: 6, of which 4 were waited for; matrix products, arithmetic and copies ran while one was open for 0% of the time, Pallas kernels for 0%

commit v1 on v0

v1 whole, which is shorter than its diff:
```python
import functools
import math

import jax
import jax.numpy as jnp
from jax import lax
from jax.experimental import pallas as pl
from jax.experimental.pallas import tpu as pltpu
from jax.sharding import PartitionSpec as P

courant = 0.3
lanes = 128


def neighbours(axis, periodic):
    count = lax.axis_size(axis)
    forward = [(i, i + 1) for i in range(count - 1)]
    if periodic:
        forward.append((count - 1, 0))
    return forward, [(target, source) for source, target in forward]


def wave_pair(phase, circle):
    quarter = circle // 4
    turn = lax.shift_right_arithmetic(phase + quarter // 2, int(math.log2(quarter)))
    angle = (phase - turn * quarter).astype(jnp.float32) * (2.0 * math.pi / circle)
    square = angle * angle
    sine = angle * (
        1.0
        + square * (-1.0 / 6 + square * (1.0 / 120 + square * (-1.0 / 5040 + square / 362880)))
    )
    cosine = 1.0 + square * (
        -0.5 + square * (1.0 / 24 + square * (-1.0 / 720 + square / 40320))
    )
    odd = (turn & 1) == 1
    cos_out = jnp.where(odd, sine, cosine)
    sin_out = jnp.where(odd, cosine, sine)
    cos_out = jnp.where(((turn + 1) & 2) == 2, -cos_out, cos_out)
    sin_out = jnp.where((turn & 2) == 2, -sin_out, sin_out)
    return cos_out, sin_out


def wave_table(sector, sectors, mode_local, grid_cols):
    circle = sectors * grid_cols
    modes = sectors * mode_local
    wave = lax.broadcasted_iota(jnp.int32, (modes, grid_cols), 0)
    place = lax.broadcasted_iota(jnp.int32, (modes, grid_cols), 1) + sector * grid_cols
    cosine, sine = wave_pair(wave * place, circle)
    norm = math.sqrt(2.0 / circle)
    table = jnp.stack(
        (
            (norm * cosine).reshape(sectors, mode_local, grid_cols),
            (-norm * sine).reshape(sectors, mode_local, grid_cols),
        ),
        axis=1,
    )
    return table.reshape(2 * modes, grid_cols)


def two_parts(value):
    high = value.astype(jnp.bfloat16)
    return high, (value - high.astype(jnp.float32)).astype(jnp.bfloat16)


def contract(left, right, dims):
    return lax.dot_general(left, right, (dims, ((), ())), preferred_element_type=jnp.float32)


def contract_split(left, right, dims):
    left_high, left_low = two_parts(left)
    right_high, right_low = two_parts(right)
    return (
        contract(left_high, right_high, dims)
        + contract(left_high, right_low, dims)
        + contract(left_low, right_high, dims)
    )


def as_column(row):
    count = row.shape[1]
    grid = jnp.broadcast_to(row, (count, count))
    diagonal = lax.broadcasted_iota(jnp.int32, (count, count), 0) == lax.broadcasted_iota(
        jnp.int32, (count, count), 1
    )
    return jnp.sum(jnp.where(diagonal, grid, 0.0), axis=1, keepdims=True)


def lon_lines(first, middle, last, west, east):
    columns = first.shape[1]
    place = lax.broadcasted_iota(jnp.int32, first.shape, 1)
    previous = jnp.where(place == 0, as_column(west), pltpu.roll(last, 1, 1))
    following = jnp.where(place == columns - 1, as_column(east), pltpu.roll(first, columns - 1, 1))
    return (
        0.5 * (last - middle) + 1.5 * previous,
        2.0 * (first - last),
        0.5 * (middle - first) - 1.5 * following,
    )


def lat_lines(first, middle, last, north, south):
    rows = first.shape[0]
    place = lax.broadcasted_iota(jnp.int32, first.shape, 0)
    previous = jnp.where(place == 0, north, pltpu.roll(last, 1, 0))
    following = jnp.where(place == rows - 1, south, pltpu.roll(first, rows - 1, 0))
    return (
        0.5 * (last - middle) + 1.5 * previous,
        2.0 * (first - last),
        0.5 * (middle - first) - 1.5 * following,
    )


def wet_of(wet_ref, sea_ref):
    return (wet_ref[...] * sea_ref[...]).astype(jnp.float32)


def source_kernel(
    sectors,
    mode_local,
    east_ref,
    north_ref,
    wet_ref,
    sea_ref,
    west_halo,
    east_halo,
    north_halo,
    south_halo,
    index_ref,
    source_ref,
    partial_ref,
    sampled_ref,
):
    wet = wet_of(wet_ref, sea_ref)
    cell_rows, cell_cols = wet.shape
    chunks = cell_cols // lanes
    for a in range(3):
        lines = lon_lines(
            *(wet * east_ref[a, b] for b in range(3)),
            west_halo[0, a : a + 1, :],
            east_halo[0, a : a + 1, :],
        )
        for b in range(3):
            for t in range(chunks):
                source_ref[(3 * a + b) * chunks + t] = lines[b][:, t * lanes : (t + 1) * lanes]
    for b in range(3):
        lines = lat_lines(
            *(wet * north_ref[a, b] for a in range(3)),
            north_halo[0, b : b + 1, :],
            south_halo[0, b : b + 1, :],
        )
        for a in range(3):
            for t in range(chunks):
                source_ref[(3 * a + b) * chunks + t] += lines[a][:, t * lanes : (t + 1) * lanes]

    grid_rows, grid_cols = index_ref.shape
    per_row = grid_rows // cell_rows
    stride = cell_rows * cell_cols // lanes

    def sample_row(row, carry):
        points = pl.ds(pl.multiple_of(row * per_row, per_row), per_row)
        place = index_ref[points, :] - row * cell_cols
        chunk = lax.shift_right_arithmetic(place, 7)
        lane = place & (lanes - 1)
        total = jnp.zeros(place.shape, jnp.float32)
        for node in range(9):
            for t in range(chunks):
                line = source_ref[node * chunks + t, pl.ds(row, 1), :]
                picked = jnp.take_along_axis(
                    jnp.broadcast_to(line, (per_row, lanes)), lane, axis=1
                )
                total = jnp.where(chunk == node * stride + t, picked, total)
        sampled_ref[points, :] = total
        return carry

    lax.fori_loop(0, cell_rows, sample_row, 0)
    table = wave_table(lax.axis_index("lon"), sectors, mode_local, grid_cols)
    partial_ref[...] = contract_split(table, sampled_ref[...], ((1,), (1,))).reshape(
        partial_ref.shape
    )


def only_mode(values, mode, mode_local):
    row = lax.broadcasted_iota(jnp.int32, values.shape, 0)
    return jnp.where(lax.rem(row, mode_local) == mode, values, 0.0).astype(jnp.bfloat16)


def analysis_kernel(spectrum_ref, legendre_ref, coeffs_ref):
    mode_local = legendre_ref.shape[0]
    spectrum = spectrum_ref[...].astype(jnp.bfloat16).astype(jnp.float32)
    degrees = legendre_ref.shape[1]
    step = 512
    for start in range(0, degrees, step):
        total = None
        for mode in range(mode_local):
            term = contract(
                only_mode(spectrum, mode, mode_local),
                legendre_ref[mode, start : start + step, :],
                ((1,), (1,)),
            )
            total = term if total is None else total + term
        coeffs_ref[:, start : start + step] = total


def synthesis_kernel(coeffs_ref, gain_ref, legendre_ref, synthesis_ref):
    mode_local = legendre_ref.shape[0]
    coeffs = coeffs_ref[...]
    wave = lax.rem(lax.broadcasted_iota(jnp.int32, coeffs.shape, 0), mode_local)
    wave = wave + lax.axis_index("lon") * mode_local
    degree = lax.broadcasted_iota(jnp.int32, coeffs.shape, 1)
    scaled = jnp.where(degree >= wave, coeffs * gain_ref[...], 0.0)
    total = None
    for mode in range(mode_local):
        term = contract(
            only_mode(scaled, mode, mode_local), legendre_ref[mode], ((1,), (0,))
        )
        total = term if total is None else total + term
    synthesis_ref[...] = total


def height_kernel(
    sectors,
    mode_local,
    pieces_ref,
    index_ref,
    height_ref,
    source_ref,
    out_ref,
    field_ref,
    left_ref,
    right_ref,
    sums_ref,
):
    grid_rows, grid_cols = index_ref.shape
    cell_rows, cell_cols = height_ref.shape[2:]
    per_row = grid_rows // cell_rows
    chunks = cell_cols // lanes
    stride = cell_rows * cell_cols // lanes
    table = wave_table(lax.axis_index("lon"), sectors, mode_local, grid_cols)
    pieces = pieces_ref[...].reshape(2 * sectors * mode_local, grid_rows)
    field_ref[...] = contract_split(pieces, table, ((0,), (0,)))
    slots = left_ref.shape[0]
    slot = lax.broadcasted_iota(jnp.int32, (slots, lanes), 0)
    code = jnp.where(slot < 9 * chunks, slot // chunks * stride + slot % chunks, -1)
    lane_code = lax.broadcasted_iota(jnp.int32, (lanes, lanes), 0)

    def add_row(row, carry):
        for g in range(per_row):
            spot = row * per_row + g
            place = index_ref[pl.ds(spot, 1), :] - row * cell_cols
            chunk = lax.shift_right_arithmetic(place, 7)
            lane = place & (lanes - 1)
            value = field_ref[pl.ds(spot, 1), :]
            high = value.astype(jnp.bfloat16).astype(jnp.float32)
            low = value - high
            here = slice(g * lanes, (g + 1) * lanes)
            left_ref[:, here] = jnp.where(chunk == code, 1.0, 0.0).astype(jnp.bfloat16)
            match = lane == lane_code
            right_ref[:lanes, here] = jnp.where(match, high, 0.0).astype(jnp.bfloat16)
            right_ref[lanes:, here] = jnp.where(match, low, 0.0).astype(jnp.bfloat16)
        both = contract(left_ref[...], right_ref[...], ((1,), (1,)))
        sums_ref[row] = both[:, :lanes] + both[:, lanes:]
        return carry

    lax.fori_loop(0, cell_rows, add_row, 0)
    for node in range(9):
        for t in range(chunks):
            here = slice(t * lanes, (t + 1) * lanes)
            loaded = sums_ref[:, node * chunks + t, :]
            out_ref[node // 3, node % 3, :, here] = height_ref[
                node // 3, node % 3, :, here
            ] - courant * (source_ref[node * chunks + t] - loaded)


def flow_kernel(
    height_ref,
    east_ref,
    north_ref,
    flow_east_ref,
    flow_north_ref,
    depth_ref,
    friction_ref,
    wet_ref,
    sea_ref,
    grad_depth_ref,
    grad_friction_ref,
    west_halo,
    east_halo,
    north_halo,
    south_halo,
    new_east_ref,
    new_north_ref,
    depth_grad_ref,
    friction_grad_ref,
):
    wet = wet_of(wet_ref, sea_ref)
    retain = wet * (1.0 - courant * friction_ref[...])
    drag = jnp.zeros_like(wet)
    for a in range(3):
        lines = lon_lines(
            *(wet * height_ref[a, b] for b in range(3)),
            west_halo[1, a : a + 1, :],
            east_halo[1, a : a + 1, :],
        )
        for b in range(3):
            east = east_ref[a, b]
            flow = flow_east_ref[a, b]
            new_east_ref[a, b] = retain * east - courant * depth_ref[a, b] * wet * lines[b]
            depth_grad_ref[a, b] = grad_depth_ref[a, b] - courant * wet * (flow * lines[b])
            drag = drag + flow * east
    for b in range(3):
        lines = lat_lines(
            *(wet * height_ref[a, b] for a in range(3)),
            north_halo[1, b : b + 1, :],
            south_halo[1, b : b + 1, :],
        )
        for a in range(3):
            north = north_ref[a, b]
            flow = flow_north_ref[a, b]
            new_north_ref[a, b] = retain * north - courant * depth_ref[a, b] * wet * lines[a]
            depth_grad_ref[a, b] -= courant * wet * (flow * lines[a])
            drag = drag + flow * north
    friction_grad_ref[...] = grad_friction_ref[...] - courant * wet * drag


def shaped(shape, dtype=jnp.float32):
    return jax.ShapeDtypeStruct(shape, dtype)


def cost(flops, bytes_accessed):
    return pl.CostEstimate(flops=flops, bytes_accessed=bytes_accessed, transcendentals=0)


def params(mebibytes):
    return pltpu.CompilerParams(vmem_limit_bytes=mebibytes << 20)


def local(
    adj_height,
    adj_east,
    adj_north,
    flow_east,
    flow_north,
    depth,
    friction,
    wet_dry,
    sea_mask,
    grad_depth,
    grad_friction,
    gauss_index,
    legendre,
    love_gain,
):
    sectors = lax.axis_size("lon")
    mode_local, degrees, grid_rows = legendre.shape
    grid_cols = gauss_index.shape[1]
    cell_rows, cell_cols = wet_dry.shape
    nodes = adj_height.shape

    wet = (wet_dry * sea_mask).astype(jnp.float32)
    forward, backward = neighbours("lon", True)
    east_height = (adj_east, adj_height)
    west_halo = lax.ppermute(
        jnp.stack([wet[:, -1] * field[:, 2, :, -1] for field in east_height]), "lon", forward
    )
    east_halo = lax.ppermute(
        jnp.stack([wet[:, 0] * field[:, 0, :, 0] for field in east_height]), "lon", backward
    )
    forward, backward = neighbours("lat", False)
    north_height = (adj_north, adj_height)
    north_halo = lax.ppermute(
        jnp.stack([wet[-1] * field[2, :, -1, :] for field in north_height]), "lat", forward
    )
    south_halo = lax.ppermute(
        jnp.stack([wet[0] * field[0, :, 0, :] for field in north_height]), "lat", backward
    )
    halos = (west_halo, east_halo, north_halo, south_halo)

    source, partial = pl.pallas_call(
        functools.partial(source_kernel, sectors, mode_local),
        out_shape=(
            shaped((9 * cell_cols // lanes, cell_rows, lanes)),
            shaped((sectors, 2 * mode_local, grid_rows)),
        ),
        scratch_shapes=[pltpu.VMEM((grid_rows, grid_cols), jnp.float32)],
        cost_estimate=cost(200_000_000, 3_000_000),
        compiler_params=params(24),
        name="source_sampled",
    )(adj_east, adj_north, wet_dry, sea_mask, *halos, gauss_index)

    spectrum = lax.psum_scatter(partial, "lon", scatter_dimension=0, tiled=True)
    spectrum = spectrum.reshape(2 * mode_local, grid_rows)

    new_east, new_north, depth_grad, friction_grad = pl.pallas_call(
        flow_kernel,
        out_shape=(shaped(nodes), shaped(nodes), shaped(nodes), shaped(wet.shape)),
        cost_estimate=cost(20_000_000, 5_000_000),
        compiler_params=params(24),
        name="flow_terms",
    )(
        adj_height,
        adj_east,
        adj_north,
        flow_east,
        flow_north,
        depth,
        friction,
        wet_dry,
        sea_mask,
        grad_depth,
        grad_friction,
        *halos,
    )

    coeffs = pl.pallas_call(
        analysis_kernel,
        out_shape=shaped((2 * mode_local, degrees)),
        cost_estimate=cost(200_000_000, 8_000_000),
        compiler_params=params(24),
        name="legendre_analysis",
    )(spectrum, legendre)
    coeffs = lax.psum(coeffs, "lat")
    synthesis = pl.pallas_call(
        synthesis_kernel,
        out_shape=shaped((2 * mode_local, grid_rows)),
        cost_estimate=cost(200_000_000, 8_000_000),
        compiler_params=params(24),
        name="legendre_synthesis",
    )(coeffs, love_gain.reshape(1, degrees), legendre)
    pieces = lax.all_gather(synthesis, "lon", axis=0, tiled=False)
    slots = 9 * cell_cols // lanes + 10
    points = grid_rows // cell_rows * lanes
    new_height = pl.pallas_call(
        functools.partial(height_kernel, sectors, mode_local),
        out_shape=shaped(nodes),
        scratch_shapes=[
            pltpu.VMEM((grid_rows, grid_cols), jnp.float32),
            pltpu.VMEM((slots, points), jnp.bfloat16),
            pltpu.VMEM((2 * lanes, points), jnp.bfloat16),
            pltpu.VMEM((cell_rows, slots, lanes), jnp.float32),
        ],
        cost_estimate=cost(200_000_000, 3_000_000),
        compiler_params=params(24),
        name="height_loaded",
    )(pieces, gauss_index, adj_height, source)
    return (new_height, new_east, new_north, depth_grad, friction_grad)


def solution(mesh):
    field = P(None, None, "lat", "lon")
    cell = P("lat", "lon")
    in_specs = (
        field,
        field,
        field,
        field,
        field,
        field,
        cell,
        cell,
        cell,
        field,
        cell,
        cell,
        P("lon", None, "lat"),
        P(),
    )
    out_specs = (field, field, field, field, cell)
    return jax.shard_map(local, mesh=mesh, in_specs=in_specs, out_specs=out_specs, check_vma=False)
```

time: 780 us -> 308 us (0.39)
  other arithmetic: 452 us -> 0.91 us
  Pallas kernels: 0 us -> 21.3 us
  local copies, waits for them, and re-layouts: 38 us -> 17.7 us
  matrix products: 15.2 us -> 0 us
    reduce_sum x33 -> x0, other arithmetic: 439 us -> none  [the longest x16 318 us: gather_block(): return jnp.sum(jnp.where(matches, block_field[:, None], 0.0), axis=0)]
    dynamic_update_slice x32 -> x0, local copies, waits for them, and re-layouts: 30.8 us -> none  [the longest x16 27.5 us: loading(): summed = lax.map(gather_block, (index_blocks, field_blocks))]
    pallas_call x0 -> x5, Pallas kernels: none -> 21.3 us  [the longest x1 11.1 us: local(): pl.pallas_call(functools.partial(height_kernel, sectors, mode_local), out...]
    dot_general x6 -> x0, matrix products: 15.2 us -> none  [the longest x1 6.31 us: loading(): jnp.einsum('kja,kla->kjl', rounded, legendre, preferred_element_type=jnp....]
    unnamed x15 -> x48, local copies, waits for them, and re-layouts: 0.07 us -> 13.7 us
  transfers between devices with their start and end apart: 6 -> 6, of which waited for: 4 -> 4; matrix products, arithmetic and copies ran while one was open for 0% -> 1% of each run, Pallas kernels for 0% -> 1%
where the time goes in v1:
time: 308 us; the launch traced here: 307 us
  waiting for transfers between devices  204 us (66%)
  blocking collectives  41 us (13%)
  Pallas kernels  21.3 us (7%)
  local copies, waits for them, and re-layouts  17.7 us (6%)
  between operations  14.3 us (5%)
  starting transfers between devices  7.33 us (2%)
    reduce_scatter x1, waiting for transfers between devices, local(): spectrum = lax.psum_scatter(partial, 'lon', scatter_dimension=0, tiled=True)  118 us
    psum x1, waiting for transfers between devices, local(): coeffs = lax.psum(coeffs, 'lat')  83.6 us
    all_gather x1, blocking collectives, local(): pieces = lax.all_gather(synthesis, 'lon', axis=0, tiled=False)  41 us
    unnamed x48, local copies, waits for them, and re-layouts  13.7 us
    pallas_call x1, Pallas kernels, local(): pl.pallas_call(functools.partial(height_kernel, sectors, mode_local), out...  11.1 us
  transfers between devices with their start and end apart: 6, of which 4 were waited for; matrix products, arithmetic and copies ran while one was open for 1% of the time, Pallas kernels for 1%

profile of v1, /device:TPU:1, one launch (start us, length us, event | category | flops | bytes accessed | tf_op | source)
XLA Modules:
  0.0 307.1 jit_solution(1292495380874527920)
XLA Ops:
  7.2 0.0 copy-start.2
  7.2 0.0 copy-start.16
  7.2 0.0 copy-start.14
  7.2 0.0 copy-start.20
  7.2 0.0 copy-start.23
  7.2 0.0 reduce-scatter.2.cloned.1.call-start
  7.3 1.0 slice_reduce_fusion.1
  8.2 0.9 slice_reduce_fusion
  9.1 0.9 multiply_convert_fusion
  10.0 0.2 slice_reduce_fusion.4
  10.2 2.8 collective-permute-start
  13.0 0.9 fusion.5
  13.9 0.9 fusion.4
  14.9 3.1 %collective-permute-start.2 = (f32[2,3,768]{2,1,0:T(4,128)S(1)}, f32[2,3,768]{2,1,0:T(4,128)S(1)}, u32[]{:S(2)}, u32[]{:S(2)}) collective-permute-start(f32[2,3,768]{2,1,0:T(4,128)S(1)} %pad_maximum_fusion), channel_id=1, source_target_pairs={{0,32},{32,64},{64,96},{96,128},{128,160},{160,192},{192,224},{1,3... | collective-permute-start | bytes 55304 | tf_op jit(solution)/shard_map/ppermute | solution.py:369
  18.1 1.3 collective-permute-start.3
  19.4 0.1 collective-permute-start.1
  19.5 0.0 collective-permute-done.west_halo
  19.5 3.0 collective-permute-done.1.east_halo
  22.5 0.0 collective-permute-done.2.north_halo
  22.5 0.1 collective-permute-done.3.south_halo
  22.6 1.0 copy-done.3
  23.6 0.0 copy-start.5
  23.6 1.0 copy-done.5
  24.7 0.0 copy-start.7
  24.7 0.9 copy-done.7
  25.6 0.0 copy-start.13
  25.6 0.8 copy-done.13
  26.4 0.0 copy-start.15
  26.4 0.8 copy-done.15
  27.2 0.0 copy-start.4
  27.2 0.0 copy-start.6
  27.2 0.0 copy-start.9
  27.2 0.0 copy-start.21
  27.2 4.5 %source_sampled.1 = (f32[54,16,128]{2,1,0:T(8,128)S(1)}, f32[32,16,256]{2,1,0:T(8,128)}) custom-call(f32[3,3,16,768]{3,2,1,0:T(8,128)S(1)} %copy-done.3, f32[3,3,16,768]{3,2,1,0:T(8,128)S(1)} %copy-done.5, s32[16,768]{1,0:T(8,128)S(1)} %copy-done.13, s32[16,768]{1,0:T(8,128)S(1)} %copy-done.15, f32[2,3,16]{2,1,0:T(4,128)S(1)} %collective-permute-done.west_halo, ...), custom_call_target="tpu_custom_call" | custom-call | flops 200000000 | bytes 3000000 | tf_op jit(solution)/shard_map/source_sampled/pallas_call | solution.py:377
  31.7 0.0 copy-start.17
  31.7 0.8 copy-done.17
  32.5 0.0 reduce-scatter.2.cloned.1.call-update
  32.5 0.0 all-reduce.2.cloned.1.call-start
  32.5 117.7 %reduce-scatter.2.cloned.1.call-done = f32[1,16,256]{2,1,0:T(8,128)} async-done(((f32[32,16,256]{2,1,0:T(8,128)}), f32[1,16,256]{2,1,0:T(8,128)}) %reduce-scatter.2.cloned.1.call-update) | async-done | bytes 16400 | tf_op jit(solution)/shard_map/reduce_scatter | solution.py:389
  150.3 3.4 %copy-done = bf16[8,2048,256]{2,1,0:T(8,128)(2,1)S(1)} copy-done((bf16[8,2048,256]{2,1,0:T(8,128)(2,1)S(1)}, bf16[8,2048,256]{2,1,0:T(8,128)(2,1)}, u32[]{:S(2)}) %copy-start) | copy-done | bytes 8388632
  153.7 0.7 copy-done.22
  154.4 2.9 legendre_analysis.1
  157.3 0.0 all-reduce.2.cloned.1.call-update
  157.4 0.0 copy-done.2
  157.4 0.0 copy-done.16
  157.4 0.0 copy-done.14
  157.4 0.0 copy-done.20
  157.4 0.0 copy-done.4
  157.4 0.0 copy-done.6
  157.4 0.0 copy-done.9
  157.4 0.0 copy-done.21
  157.4 0.0 copy-done.10
  157.4 0.0 copy-done.11
  157.5 0.0 copy-done.12
  157.5 1.6 flow_terms.1
  159.0 83.6 %all-reduce.2.cloned.1.call-done.coeffs_ref = f32[16,2048]{1,0:T(8,128)} async-done(((f32[16,2048]{1,0:T(8,128)}), f32[16,2048]{1,0:T(8,128)}) %all-reduce.2.cloned.1.call-update) | async-done | bytes 131088 | tf_op jit(solution)/shard_map/psum | solution.py:420
  242.6 0.0 copy-done.23
  242.6 3.4 %copy-done.1 = bf16[8,2048,256]{2,1,0:T(8,128)(2,1)S(1)} copy-done((bf16[8,2048,256]{2,1,0:T(8,128)(2,1)S(1)}, bf16[8,2048,256]{2,1,0:T(8,128)(2,1)}, u32[]{:S(2)}) %copy-start.1) | copy-done | bytes 8388632
  246.0 0.9 copy-done.19
  246.9 1.2 legendre_synthesis.1
  248.1 41.0 %all-gather = f32[512,256]{1,0:T(8,128)S(1)} all-gather(f32[16,256]{1,0:T(8,128)S(1)} %legendre_synthesis.1), channel_id=2, replica_groups=mesh['lat'=8,'lon'=32] {'lon'}, dimensions={0}, use_global_device_ids=true | all-gather | bytes 540672 | tf_op jit(solution)/shard_map/all_gather | solution.py:428
  289.1 0.0 copy-done.8
  289.1 0.0 copy-done.18
  289.1 11.1 %height_loaded.1 = f32[3,3,16,768]{3,2,1,0:T(8,128)} custom-call(f32[32,16,256]{2,1,0:T(8,128)S(1)} %bitcast.27, s32[256,128]{1,0:T(8,128)S(1)} %copy-done.8, f32[3,3,16,768]{3,2,1,0:T(8,128)S(1)} %copy-done.2, f32[54,16,128]{2,1,0:T(8,128)S(1)} %copy-done.18), custom_call_target="tpu_custom_call" | custom-call | flops 200000000 | bytes 3000000 | tf_op jit(solution)/shard_map/height_loaded/pallas_call | solution.py:431
  (17 shorter events, 0.1 us)
Async XLA Ops:
  7.2 150.2 %copy-start.2 = (f32[3,3,16,768]{3,2,1,0:T(8,128)S(1)}, f32[3,3,16,768]{3,2,1,0:T(8,128)}, u32[]{:S(2)}) copy-start(f32[3,3,16,768]{3,2,1,0:T(8,128)} %height_ref.3) | copy-start | bytes 1327108
  7.2 150.2 %copy-start.16 = (s32[16,768]{1,0:T(8,128)S(1)}, s32[16,768]{1,0:T(8,128)}, u32[]{:S(2)}) copy-start(s32[16,768]{1,0:T(8,128)} %sea_ref.3) | copy-start | bytes 147460
  7.2 150.2 %copy-start.14 = (s32[16,768]{1,0:T(8,128)S(1)}, s32[16,768]{1,0:T(8,128)}, u32[]{:S(2)}) copy-start(s32[16,768]{1,0:T(8,128)} %wet_ref.3) | copy-start | bytes 147460
  7.2 150.2 %copy-start.20 = (f32[16,768]{1,0:T(8,128)S(1)}, f32[16,768]{1,0:T(8,128)}, u32[]{:S(2)}) copy-start(f32[16,768]{1,0:T(8,128)} %friction_ref.1) | copy-start | bytes 147460
  7.2 235.4 %copy-start.23 = (f32[2048]{0:T(1024)S(1)}, f32[2048]{0:T(1024)}, u32[]{:S(2)}) copy-start(f32[2048]{0:T(1024)} %param.27) | copy-start | bytes 24580
  7.2 143.1 %reduce-scatter.2.cloned.1.call-start = ((), (), s32[]{:S(2)}) async-start(), calls=%async_computation.1 | async-start | bytes 540672 | tf_op jit(solution)/shard_map/reduce_scatter | solution.py:389
  10.2 9.3 %collective-permute-start = (f32[2,3,16]{2,1,0:T(4,128)S(1)}, f32[2,3,16]{2,1,0:T(4,128)S(1)}, u32[]{:S(2)}, u32[]{:S(2)}) collective-permute-start(f32[2,3,16]{2,1,0:T(4,128)S(1)} %pad_maximum_fusion.2), channel_id=1, source_target_pairs={{0,1},{1,2},{2,3},{3,4},{4,5},{5,6},{6,7},{7,8},{8,9},{9,10},{10,1... | collective-permute-start | bytes 1160 | tf_op jit(solution)/shard_map/ppermute | solution.py:361
  14.9 7.6 %collective-permute-start.2 = (f32[2,3,768]{2,1,0:T(4,128)S(1)}, f32[2,3,768]{2,1,0:T(4,128)S(1)}, u32[]{:S(2)}, u32[]{:S(2)}) collective-permute-start(f32[2,3,768]{2,1,0:T(4,128)S(1)} %pad_maximum_fusion), channel_id=1, source_target_pairs={{0,32},{32,64},{64,96},{96,128},{128,160},{160,192},{192,224},{1,3... | collective-permute-start | bytes 55304 | tf_op jit(solution)/shard_map/ppermute | solution.py:369
  18.1 4.6 %collective-permute-start.3 = (f32[2,3,768]{2,1,0:T(4,128)S(1)}, f32[2,3,768]{2,1,0:T(4,128)S(1)}, u32[]{:S(2)}, u32[]{:S(2)}) collective-permute-start(f32[2,3,768]{2,1,0:T(4,128)S(1)} %pad_maximum_fusion.1), channel_id=1, source_target_pairs={{32,0},{64,32},{96,64},{128,96},{160,128},{192,160},{224,192},{33,... | collective-permute-start | bytes 55304 | tf_op jit(solution)/shard_map/ppermute | solution.py:372
  19.4 3.1 %collective-permute-start.1 = (f32[2,3,16]{2,1,0:T(4,128)S(1)}, f32[2,3,16]{2,1,0:T(4,128)S(1)}, u32[]{:S(2)}, u32[]{:S(2)}) collective-permute-start(f32[2,3,16]{2,1,0:T(4,128)S(1)} %pad_maximum_fusion.3), channel_id=1, source_target_pairs={{1,0},{2,1},{3,2},{4,3},{5,4},{6,5},{7,6},{8,7},{9,8},{10,9},{11,1... | collective-permute-start | bytes 1160 | tf_op jit(solution)/shard_map/ppermute | solution.py:364
  22.6 1.0 copy-start.3
  23.6 1.0 copy-start.5
  24.7 0.9 copy-start.7
  25.6 0.8 copy-start.13
  26.4 0.8 copy-start.15
  27.2 130.2 %copy-start.4 = (f32[3,3,16,768]{3,2,1,0:T(8,128)S(1)}, f32[3,3,16,768]{3,2,1,0:T(8,128)}, u32[]{:S(2)}) copy-start(f32[3,3,16,768]{3,2,1,0:T(8,128)} %east_ref.3) | copy-start | bytes 1327108
  27.2 130.2 %copy-start.6 = (f32[3,3,16,768]{3,2,1,0:T(8,128)S(1)}, f32[3,3,16,768]{3,2,1,0:T(8,128)}, u32[]{:S(2)}) copy-start(f32[3,3,16,768]{3,2,1,0:T(8,128)} %north_ref.3) | copy-start | bytes 1327108
  27.2 130.2 %copy-start.9 = (f32[3,3,16,768]{3,2,1,0:T(8,128)S(1)}, f32[3,3,16,768]{3,2,1,0:T(8,128)}, u32[]{:S(2)}) copy-start(f32[3,3,16,768]{3,2,1,0:T(8,128)} %flow_east_ref.1) | copy-start | bytes 1327108
  27.2 130.3 %copy-start.21 = (f32[16,768]{1,0:T(8,128)S(1)}, f32[16,768]{1,0:T(8,128)}, u32[]{:S(2)}) copy-start(f32[16,768]{1,0:T(8,128)} %grad_friction_ref.1) | copy-start | bytes 147460
  31.7 0.8 copy-start.17
  32.5 210.1 %all-reduce.2.cloned.1.call-start = ((), (), s32[]{:S(2)}) async-start(), calls=%async_computation.2 | async-start | bytes 262144 | tf_op jit(solution)/shard_map/psum | solution.py:420
  150.3 3.4 %copy-start = (bf16[8,2048,256]{2,1,0:T(8,128)(2,1)S(1)}, bf16[8,2048,256]{2,1,0:T(8,128)(2,1)}, u32[]{:S(2)}) copy-start(bf16[8,2048,256]{2,1,0:T(8,128)(2,1)} %legendre_ref.3) | copy-start | bytes 25165828
  153.7 0.7 copy-start.22
  154.4 3.0 copy-start.10
  154.4 3.0 copy-start.11
  154.4 3.1 copy-start.12
  157.3 131.8 %copy-start.8 = (s32[256,128]{1,0:T(8,128)S(1)}, s32[256,128]{1,0:T(8,128)}, u32[]{:S(2)}) copy-start(s32[256,128]{1,0:T(8,128)} %index_ref.3) | copy-start | bytes 393220
  242.6 3.4 %copy-start.1 = (bf16[8,2048,256]{2,1,0:T(8,128)(2,1)S(1)}, bf16[8,2048,256]{2,1,0:T(8,128)(2,1)}, u32[]{:S(2)}) copy-start(bf16[8,2048,256]{2,1,0:T(8,128)(2,1)} %legendre_ref.3) | copy-start | bytes 25165828
  246.0 0.9 copy-start.19
  246.9 42.2 %copy-start.18 = (f32[54,16,128]{2,1,0:T(8,128)S(1)}, f32[54,16,128]{2,1,0:T(8,128)}, u32[]{:S(2)}) copy-start(f32[54,16,128]{2,1,0:T(8,128)} %copy-done.17) | copy-start | bytes 1327108
Sparse Core Ops, SparseCore 0:
  32.6 117.6 reduce-scatter.1
  157.5 85.0 all-reduce.1
